TPU v7x, 256 devices: a whole 4x4x8 slice. The times are simulated.
256 devices in a mesh: wide: 32 (over x, z_hi, core), narrow: 8 (over z_lo, y).
Axes of the slice: x: 4, y: 4, z: 8 (z_hi: 4, z_lo: 2; z = z_hi * 2 + z_lo), core: 2. Of those that a mesh axis runs over, the one named last changes fastest.
Arguments:
- acts: bfloat16 [4096, 4096], P('wide', 'narrow'), may hold values from -6 to 6
- grads: bfloat16 [4096, 14336], P('wide', 'narrow'), may hold values from -6 to 6
- basis_a: bfloat16 [4096, 4096], P(None, 'narrow'), may hold values from -4 to 4
- basis_g: bfloat16 [14336, 14336], P('narrow', 'wide'), may hold values from -4 to 4
- source_of_block: int32 [32, 1], replicated, may hold values from 0 to 15
- probe_blocks: int32 [1024, 2], replicated, may hold values from 0 to 31, all different within a row
Outputs:
- correction: float32 [4096, 14336], P('narrow', 'wide')
- influence: float32 [1024, 16], replicated
Inputs may be any that keep to these rules, and one draw needn't show every extreme that they name: `probe_blocks`: each probe pair names two different blocks; every block is named by some pair. `source_of_block`: every source owns at least one block.
All inputs are finite; a program needn't handle non-finite values.
Results may differ from a plain program's by a relative error of at most 0.005.
Values may be sent and summed in bfloat16 or wider, within the bound.
A program may use at most 128 MiB of HBM per device.

v0:
```python
import functools
import math

import jax
import jax.numpy as jnp
from jax import lax
from jax.experimental import pallas as pl
from jax.experimental.pallas import tpu as pltpu
from jax.sharding import PartitionSpec as P

D = 4096
FF = 14336
BLOCK = 128
SOURCES = 16
NB = 32
TOKENS = 4096
ROWS = D // 8
COLS = FF // 32
MESH = pl.DeviceIdType.MESH
NT = (((1,), (1,)), ((), ()))
STAGES = (16, 16)


def stage_peers():
    w, n = lax.axis_index("wide"), lax.axis_index("narrow")
    near, far = (w % 2) * 8 + n, w // 2

    def peer(stage, d):
        if stage == 0:
            other = (near + d) % 16
            return (far * 2 + other // 8, other % 8)
        return (((far + d) % 16) * 2 + w % 2, n)

    return peer, (near, far)


def sum_copy(stage, slots, send, recv, source, d):
    peer, _ = stage_peers()
    return pltpu.make_async_remote_copy(
        src_ref=slots.at[source],
        dst_ref=slots.at[source],
        send_sem=send,
        recv_sem=recv,
        device_id=peer(stage, d),
        device_id_type=MESH,
    )


def sum_begin(stage, value, slots, send, recv):
    mine = stage_peers()[1][stage]
    slots[mine] = value
    for d in range(1, STAGES[stage]):
        sum_copy(stage, slots, send, recv, mine, d).start()


def sum_end(stage, slots, send, recv):
    size = STAGES[stage]
    sum_copy(stage, slots, send, recv, pl.ds(0, size - 1), 1).wait()
    total = slots[0]
    for s in range(1, size):
        total = total + slots[s]
    return total


EVENTS = (
    (0, 0), (-1, 0), (1, 0), (0, -1), (0, 1), (2, 0), (0, 2), (-1, -1),
    (1, -1), (-1, 1), (1, 1), (2, -1), (2, 1), (-1, 2), (1, 2), (2, 2),
)
STEPS = len(EVENTS)
R_STEPS = (6,) + tuple(range(9, 24))
ORDER = 1
ENERGY_STEP = 8
SUM_LAG = 3
RESULT_LAG = 6
PASS_LAG = 8
USE_STEP = 17
HALF = COLS // 2
WIDE = 7


def table(step, values):
    picked = jnp.int32(values[0])
    for index, value in enumerate(values):
        if index:
            picked = jnp.where(step == index, jnp.int32(value), picked)
    return picked


class Place:
    def __init__(self):
        self.w, self.n = lax.axis_index("wide"), lax.axis_index("narrow")
        self.x, self.z, self.c = self.w // 8, (self.w // 2) % 4, self.w % 2

    def at(self, dx, dz, c):
        return ((self.x + dx + 4) % 4) * 8 + ((self.z + dz + 4) % 4) * 2 + c

    def owned(self, event, c):
        return self.at(*EVENTS[event], c)


class Relay:
    def __init__(self, place, buffer, send, recv, other):
        self.place, self.buffer, self.send, self.recv, self.other = place, buffer, send, recv, other
        self.half = buffer.shape[1] // 2

    def part(self, chunk, which):
        if which is None:
            return self.buffer.at[chunk]
        return self.buffer.at[chunk, pl.ds(which * self.half, self.half)]

    def copy(self, event, which, slot, recv_sem, dx, dz, dc=0):
        place = self.place
        ref = self.part(place.owned(event, place.c), which)
        c = (place.c + dc) % 2
        return pltpu.make_async_remote_copy(
            src_ref=ref,
            dst_ref=ref,
            send_sem=self.send.at[event, slot],
            recv_sem=recv_sem,
            device_id=(place.at(dx, dz, c), place.n),
            device_id_type=MESH,
        )

    def sends(self, event):
        dx, dz = EVENTS[event]
        recv = self.recv
        found = []
        if dx == 0:
            found.append(self.copy(event, None, 1, recv.at[EVENTS.index((-1, dz)), 0], 1, 0))
            found.append(self.copy(event, None, 2, recv.at[EVENTS.index((1, dz)), 0], -1, 0))
        if (dx, dz) == (0, 0):
            found.append(self.copy(event, None, 3, recv.at[EVENTS.index((0, -1)), 0], 0, 1))
            found.append(self.copy(event, None, 4, recv.at[EVENTS.index((0, 1)), 0], 0, -1))
        if (dx, dz) == (0, -1):
            found.append(self.copy(event, 0, 3, recv.at[EVENTS.index((0, 2)), 0], 0, 1))
        if (dx, dz) == (0, 1):
            found.append(self.copy(event, 1, 4, recv.at[EVENTS.index((0, 2)), 1], 0, -1))
        if dx == -1:
            found.append(self.copy(event, 0, 1, recv.at[EVENTS.index((2, dz)), 0], 1, 0))
        if dx == 1:
            found.append(self.copy(event, 1, 2, recv.at[EVENTS.index((2, dz)), 1], -1, 0))
        found.append(self.copy(event, None, 0, self.other.at[event], 0, 0, 1))
        return found

    def wait_arrival(self, event):
        dx, dz = EVENTS[event]
        if (dx, dz) == (0, 0):
            return
        halves = (0, 1) if dx == 2 or dz == 2 and dx == 0 else (None,)
        for which in halves:
            self.copy(event, which, 0, self.recv.at[event, which or 0], 0, 0, 1).wait_recv()

    def step(self, event):
        self.wait_arrival(event)
        for copy in self.sends(event):
            copy.start()

    def wait_other(self, event):
        place = self.place
        dx = table(event, [e[0] for e in EVENTS])
        dz = table(event, [e[1] for e in EVENTS])
        ref = self.buffer.at[place.at(dx, dz, 1 - place.c)]
        pltpu.make_async_remote_copy(
            src_ref=ref,
            dst_ref=ref,
            send_sem=self.send.at[0, 0],
            recv_sem=self.other.at[event],
            device_id=(place.at(0, 0, 1 - place.c), place.n),
            device_id_type=MESH,
        ).wait_recv()
        return place.at(dx, dz, 0)

    def finish(self):
        for event in range(STEPS):
            for copy in self.sends(event):
                copy.wait_send()


def whole_kernel(
    acts_hbm, grads_hbm, basis_a_hbm, basis_t_hbm, source_ref, probe_ref, corr, influence,
    grads, acts, basis_a, basis_t, parts, shares, crossed, ra, rg, products, gram, recip, small, large,
    energy, weight, weight_line, weight_own,
    local, g_send, g_recv, g_other, r_send, r_recv, r_other,
    a_send, a_recv, s_send, s_recv, z_send, z_recv, b_send, b_recv, f_send, send_s, recv_s, send_l, recv_l,
    l_send, l_recv, w_send, w_recv,
):
    place = Place()
    w, n, c = place.w, place.n, place.c
    y, line = n % 4, (n // 4) * 4
    width = acts_hbm.shape[1]
    own_cols = pl.ds(pl.multiple_of(n * width, width), width)
    fetch = [
        pltpu.make_async_copy(grads_hbm, grads.at[w], local.at[0]),
        pltpu.make_async_copy(acts_hbm, acts.at[:, own_cols], local.at[1]),
        pltpu.make_async_copy(basis_t_hbm, basis_t, local.at[2]),
        pltpu.make_async_copy(basis_a_hbm, basis_a, local.at[3]),
    ]
    for copy in fetch:
        copy.start()
    peer, _ = stage_peers()
    barrier = pltpu.get_barrier_semaphore()
    count = 0
    for stage, size in enumerate(STAGES):
        for d in range(1, size):
            pl.semaphore_signal(barrier, inc=1, device_id=peer(stage, d), device_id_type=MESH)
            count += 1
    for event in range(1, STEPS):
        dx, dz = EVENTS[event]
        pl.semaphore_signal(barrier, inc=1, device_id=(place.at(dx, dz, 1 - c), n), device_id_type=MESH)
        count += 1
    pl.semaphore_wait(barrier, count)

    g_relay = Relay(place, grads, g_send, g_recv, g_other)
    r_relay = Relay(place, ra, r_send, r_recv, r_other)
    fetch[0].wait()
    g_relay.step(0)

    def acts_copy(d, source):
        cols = pl.ds(pl.multiple_of(source * width, width), width)
        return pltpu.make_async_remote_copy(
            src_ref=acts.at[:, cols],
            dst_ref=acts.at[:, cols],
            send_sem=a_send.at[d],
            recv_sem=a_recv.at[d],
            device_id=(w, (n + d) % 8),
            device_id_type=MESH,
        )

    fetch[1].wait()
    for d in range(1, 8):
        acts_copy(d, n).start()
    corr[...] = jnp.zeros_like(corr)
    gram[...] = jnp.zeros_like(gram)
    fetch[2].wait()

    def share_copy(q, source, target):
        return pltpu.make_async_remote_copy(
            src_ref=parts.at[q],
            dst_ref=shares.at[q // 4, source],
            send_sem=s_send.at[q],
            recv_sem=s_recv.at[q // 4, source],
            device_id=(w, line + target),
            device_id_type=MESH,
        )

    def line_sum(q):
        total = parts[q].astype(jnp.float32)
        for d in range(1, 4):
            total = total + shares[q // 4, (y + d) % 4].astype(jnp.float32)
        return total

    def cross_copy(q):
        return pltpu.make_async_remote_copy(
            src_ref=crossed.at[q // 4, 0],
            dst_ref=crossed.at[q // 4, 1],
            send_sem=z_send.at[q // 4],
            recv_sem=z_recv.at[q // 4],
            device_id=(w, (n + 4) % 8),
            device_id_type=MESH,
        )

    def result_copy(block, q, which, send_sem, d):
        ref = rg.at[block] if which is None else rg.at[block, pl.ds(which * HALF, HALF)]
        return pltpu.make_async_remote_copy(
            src_ref=ref,
            dst_ref=ref,
            send_sem=send_sem,
            recv_sem=b_recv.at[q, which or 0],
            device_id=(w, line + (y + d) % 4),
            device_id_type=MESH,
        )

    def first_of(event):
        return place.at(table(event, [e[0] for e in EVENTS]), table(event, [e[1] for e in EVENTS]), 0)

    def square(value):
        value = value.astype(jnp.float32)
        return (value * value).astype(jnp.bfloat16)

    def add_products(event):
        first = first_of(event)
        tiles = []
        for k in range(2):
            tile = lax.dot_general(rg[first + k], ra[first + k], NT, preferred_element_type=jnp.float32)
            tiles.append(tile.reshape(COLS // (8 * WIDE), WIDE, 1, 8, ROWS))
        both = jnp.concatenate(tiles, axis=2).astype(jnp.bfloat16).reshape(COLS // (8 * WIDE), WIDE, 16, ROWS)
        for g in range(WIDE):
            products[:, pl.ds(pl.multiple_of(first * 8, 16), 16), g * ROWS : (g + 1) * ROWS] = both[:, g]

    def line_copy(source, d):
        return pltpu.make_async_remote_copy(
            src_ref=weight_line.at[source],
            dst_ref=weight_line.at[source],
            send_sem=l_send.at[d],
            recv_sem=l_recv.at[d],
            device_id=(w, line + (y + d) % 4),
            device_id_type=MESH,
        )

    def weight_copy(event, core):
        dx, dz = EVENTS[event]
        return pltpu.make_async_remote_copy(
            src_ref=weight_own,
            dst_ref=weight.at[event // 2],
            send_sem=w_send.at[event // 2, core],
            recv_sem=w_recv.at[event // 2],
            device_id=(place.at(-dx, -dz, core), n),
            device_id_type=MESH,
        )

    def hand_out(act):
        for event in range(STEPS):
            for core in range(2):
                gives = (y % 2 == c) & (y // 2 == event % 2)
                if event == 0:
                    gives = gives & (core != c)
                pl.when(gives)(functools.partial(act, event, core))

    def weight_slots(act):
        for slot in range(8):
            if slot == 0:
                pl.when((y // 2 == 1) | (y % 2 != c))(functools.partial(act, slot))
            else:
                act(slot)

    def use(event, carry):
        first = first_of(event)
        for h in range(2):
            q = 2 * event + h

            @pl.when(q % 4 == (y + 2) % 4)
            def _():
                for which in range(2):
                    result_copy(first + h, q, which, f_send.at[q], 1).wait_recv()

        r_relay.wait_other(event)
        sa = jnp.concatenate([square(ra[first + k]) for k in range(2)], axis=1)
        sg = jnp.concatenate([square(rg[first + k]) for k in range(2)], axis=1)
        corr[...] += lax.dot_general(sg, sa, NT, preferred_element_type=jnp.float32)

        add_products(event)
        return carry

    def one_step(step, carry):
        def relay():
            for event in range(1, STEPS):
                pl.when(step == event)(functools.partial(g_relay.step, event))

        if ORDER == 0:
            relay()

        @pl.when((step >= 1) & (step <= STEPS))
        def _():
            event = step - 1
            first = g_relay.wait_other(event)
            both = grads[pl.ds(first, 2)].reshape(2 * BLOCK, grads.shape[2])
            product = lax.dot_general(basis_t[...], both, NT, preferred_element_type=jnp.float32)
            for h in range(2):
                q = 2 * event + h
                parts[q] = product[:, h * BLOCK : (h + 1) * BLOCK].astype(jnp.bfloat16)

                @pl.when(q % 4 != y)
                def _():
                    share_copy(q, y, q % 4).start()

        if ORDER == 1:
            relay()

        @pl.when((step >= SUM_LAG) & (step < STEPS + SUM_LAG))
        def _():
            event = step - SUM_LAG
            for h in range(2):
                q = 2 * event + h

                @pl.when(q % 4 == y)
                def _():
                    for d in range(1, 4):
                        share_copy(q, (y + d) % 4, (y + d) % 4).wait_recv()
                    crossed[q // 4, 0] = line_sum(q).astype(jnp.bfloat16)
                    cross_copy(q).start()

        @pl.when((step >= RESULT_LAG) & (step < STEPS + RESULT_LAG))
        def _():
            event = step - RESULT_LAG
            for h in range(2):
                q = 2 * event + h

                @pl.when(q % 4 == y)
                def _():
                    cross_copy(q).wait_recv()
                    block = first_of(event) + h
                    total = (line_sum(q) + crossed[q // 4, 1].astype(jnp.float32)).astype(jnp.bfloat16)
                    rg[block] = total
                    energy[q // 4] = jnp.sum(square(total).astype(jnp.float32).reshape(COLS // 8, 8, BLOCK), axis=0)
                    result_copy(block, q, None, b_send.at[q // 4, 0], 1).start()
                    result_copy(block, q, None, b_send.at[q // 4, 1], 3).start()

        @pl.when((step >= PASS_LAG) & (step < STEPS + PASS_LAG))
        def _():
            event = step - PASS_LAG
            for h in range(2):
                q = 2 * event + h
                block = first_of(event) + h

                @pl.when(q % 4 == (y + 3) % 4)
                def _():
                    result_copy(block, q, None, f_send.at[q], 1).wait_recv()
                    result_copy(block, q, 0, f_send.at[q], 1).start()

                @pl.when(q % 4 == (y + 1) % 4)
                def _():
                    result_copy(block, q, None, f_send.at[q], 3).wait_recv()
                    result_copy(block, q, 1, f_send.at[q], 3).start()

        @pl.when(step == R_STEPS[0])
        def _():
            fetch[3].wait()
            for d in range(1, 8):
                acts_copy(d, (n + 8 - d) % 8).wait_recv()
            turned = jnp.dot(acts[...], basis_a[...], preferred_element_type=jnp.float32)
            own = turned.T.astype(jnp.bfloat16)
            ra[w] = own
            own = jnp.sum(square(own).astype(jnp.float32).reshape(ROWS // 8, 8, BLOCK), axis=0)
            weight_line[y] = jnp.broadcast_to(jnp.sum(own, axis=0, keepdims=True), (8, BLOCK))
            for d in range(1, 4):
                line_copy(y, d).start()

        for event in range(STEPS):
            pl.when(step == (R_STEPS[event]))(functools.partial(r_relay.step, event))

        @pl.when(step == ENERGY_STEP)
        def _():
            for d in range(1, 4):
                line_copy((y + 4 - d) % 4, d).wait_recv()
            weight_own[...] = weight_line[0] + weight_line[1] + weight_line[2] + weight_line[3]
            hand_out(lambda event, core: weight_copy(event, core).start())

            @pl.when((y // 2 == 0) & (y % 2 == c))
            def _():
                weight[0] = weight_own[...]

        @pl.when(step == STEPS + RESULT_LAG - 1)
        def _():
            weight_slots(lambda slot: weight_copy(2 * slot, 0).wait_recv())
            total = jnp.zeros((8, BLOCK), jnp.float32)
            for slot in range(8):
                total = total + weight[slot] * energy[slot]
            total = jnp.full((8, 128), jnp.sum(total), jnp.float32)
            sum_begin(0, total, small.at[0], send_s.at[0], recv_s.at[0])

        @pl.when(step == STEPS + RESULT_LAG + 1)
        def _():
            total = sum_end(0, small.at[0], send_s.at[0], recv_s.at[0])
            sum_begin(1, total, small.at[1], send_s.at[1], recv_s.at[1])

        @pl.when(step >= USE_STEP)
        def _():
            lax.fori_loop(2 * (step - USE_STEP), 2 * (step - USE_STEP) + 2, use, 0)

        return carry

    lax.fori_loop(1, USE_STEP + STEPS // 2, one_step, 0)
    moments = corr[...] * (1.0 / TOKENS)
    corr[...] = moments
    total = sum_end(1, small.at[1], send_s.at[1], recv_s.at[1])
    damping = (0.1 / (float(D) * FF * TOKENS)) * total[0:1, 0:1]
    flipped = (1.0 / (moments + damping)).reshape(COLS // (8 * WIDE), WIDE, 8, ROWS)
    for g in range(WIDE):
        recip[:, :, g * ROWS : (g + 1) * ROWS] = flipped[:, g]

    def add_gram(group, carry):
        tile = products[group]
        scaled = (tile.astype(jnp.float32).reshape(NB, 8, WIDE * ROWS) * recip[group][None]).astype(jnp.bfloat16)
        gram[...] += lax.dot_general(
            scaled.reshape(NB * 8, WIDE * ROWS), tile, NT, preferred_element_type=jnp.float32
        )
        return carry

    lax.fori_loop(0, COLS // (8 * WIDE), add_gram, 0)
    size = NB * 8
    rows = lax.broadcasted_iota(jnp.int32, (size, size), 0) % 8
    cols = lax.broadcasted_iota(jnp.int32, (size, size), 1) % 8
    own = jnp.where(rows == cols, gram[...], 0.0).reshape(NB, 8, size)
    own = jnp.sum(own, axis=1)
    pick = lax.broadcasted_iota(jnp.int32, (size, 128), 0) // 8 == lax.broadcasted_iota(jnp.int32, (size, 128), 1)
    exact = dict(precision=lax.Precision.HIGHEST, preferred_element_type=jnp.float32)
    kernel_t = jnp.dot(own, pick.astype(jnp.float32), **exact)
    packed = jnp.concatenate([kernel_t[8 * k : 8 * k + 8, :NB] for k in range(4)], axis=1)
    for stage in range(2):
        sum_begin(stage, packed, large.at[stage], send_l.at[stage], recv_l.at[stage])
        packed = sum_end(stage, large.at[stage], send_l.at[stage], recv_l.at[stage])
    kernel_t = jnp.concatenate([packed[:, NB * k : NB * k + NB] for k in range(4)], axis=0)

    pairs = probe_ref.shape[1]
    ids = lax.broadcasted_iota(jnp.int32, (NB, pairs), 0)
    pick_c = (probe_ref[0:1, :] == ids).astype(jnp.float32)
    pick_r = (probe_ref[1:2, :] == ids).astype(jnp.float32)
    spread = jnp.dot(kernel_t, pick_c - pick_r, **exact)
    keep = 1.0 - pick_c - pick_r
    owner = (source_ref[...] == lax.broadcasted_iota(jnp.int32, (SOURCES, NB), 0)).astype(jnp.float32)
    factor = 1.0 / (BLOCK * math.sqrt(D * FF))
    influence[...] = jnp.dot(owner, spread * keep, **exact) * factor

    for i in range(8):
        for d in range(1, 4):
            share_copy(4 * i + (y + d) % 4, y, (y + d) % 4).wait_send()
        cross_copy(4 * i).wait_send()
        result_copy(0, 0, None, b_send.at[i, 0], 1).wait_send()
        result_copy(0, 0, None, b_send.at[i, 1], 3).wait_send()
        result_copy(0, 0, 0, f_send.at[4 * i + (y + 3) % 4], 1).wait_send()
        result_copy(0, 0, 1, f_send.at[4 * i + (y + 1) % 4], 3).wait_send()
    for d in range(1, 8):
        acts_copy(d, n).wait_send()
    for d in range(1, 4):
        line_copy(y, d).wait_send()
    hand_out(lambda event, core: weight_copy(event, core).wait_send())
    g_relay.finish()
    r_relay.finish()


def whole_call(acts, grads, basis_a, basis_t, source, probe):
    anywhere = pl.BlockSpec(memory_space=pl.ANY)
    whole = pl.BlockSpec(memory_space=pltpu.VMEM)
    dma = pltpu.SemaphoreType.DMA
    bf16, f32 = jnp.bfloat16, jnp.float32
    hidden = grads.shape[1]
    return pl.pallas_call(
        whole_kernel,
        out_shape=(
            jax.ShapeDtypeStruct((COLS, ROWS), f32),
            jax.ShapeDtypeStruct((SOURCES, probe.shape[1]), f32),
        ),
        in_specs=[anywhere] * 4 + [whole] * 2,
        out_specs=(whole, whole),
        scratch_shapes=[
            pltpu.VMEM((NB, BLOCK, hidden), bf16),
            pltpu.VMEM((BLOCK, D), bf16),
            pltpu.VMEM((D, ROWS), bf16),
            pltpu.VMEM((COLS, hidden), bf16),
            pltpu.VMEM((NB, COLS, BLOCK), bf16),
            pltpu.VMEM((8, 4, COLS, BLOCK), bf16),
            pltpu.VMEM((8, 2, COLS, BLOCK), bf16),
            pltpu.VMEM((NB, ROWS, BLOCK), bf16),
            pltpu.VMEM((NB, COLS, BLOCK), bf16),
            pltpu.VMEM((COLS // (8 * WIDE), NB * 8, WIDE * ROWS), bf16),
            pltpu.VMEM((NB * 8, NB * 8), f32),
            pltpu.VMEM((COLS // (8 * WIDE), 8, WIDE * ROWS), f32),
            pltpu.VMEM((2, 16, 8, 128), f32),
            pltpu.VMEM((2, 16, 8, 128), f32),
            pltpu.VMEM((8, 8, 128), f32),
            pltpu.VMEM((8, 8, 128), f32),
            pltpu.VMEM((4, 8, 128), f32),
            pltpu.VMEM((8, 128), f32),
            dma((4,)),
            dma((STEPS, 5)),
            dma((STEPS, 2)),
            dma((STEPS,)),
            dma((STEPS, 5)),
            dma((STEPS, 2)),
            dma((STEPS,)),
            dma((8,)),
            dma((8,)),
            dma((NB,)),
            dma((8, 4)),
            dma((8,)),
            dma((8,)),
            dma((8, 2)),
            dma((NB, 2)),
            dma((NB,)),
            dma((2,)),
            dma((2,)),
            dma((2,)),
            dma((2,)),
            dma((4,)),
            dma((4,)),
            dma((8, 2)),
            dma((8,)),
        ],
        compiler_params=pltpu.CompilerParams(
            collective_id=1, has_side_effects=True, vmem_limit_bytes=60 * 1024 * 1024
        ),
        cost_estimate=pl.CostEstimate(flops=10**10, bytes_accessed=10**7, transcendentals=0),
    )(acts, grads, basis_a, basis_t, source, probe)


def on_device(acts, grads, basis_a, basis_g, source_of_block, probe_blocks):
    correction, influence = whole_call(
        acts, grads, basis_a, basis_g.T, source_of_block.T, probe_blocks.T
    )
    return (correction.T, influence.T)


def solution(mesh):
    placed = (
        P("wide", "narrow"),
        P("wide", "narrow"),
        P(None, "narrow"),
        P("narrow", "wide"),
        P(),
        P(),
    )
    return jax.shard_map(
        on_device, mesh=mesh, in_specs=placed, out_specs=(P("narrow", "wide"), P()), check_vma=False
    )
```

profile of v0, /device:TPU:1, one launch (start us, length us, event | category | flops | bytes accessed | tf_op | source)
XLA Modules:
  0.0 151.8 jit_solution(17846281747085409830)
XLA Ops:
  0.6 147.5 %shard_map.77 = (f32[448,512]{1,0:T(8,128)}, f32[16,1024]{1,0:T(8,128)}) custom-call(bf16[128,512]{1,0:T(8,128)(2,1)} %acts_hbm.1, bf16[128,1792]{1,0:T(8,128)(2,1)} %grads_hbm.1, bf16[4096,512]{1,0:T(8,128)(2,1)} %basis_a_hbm.1, bf16[448,1792]{1,0:T(8,128)(2,1)} %bitcast.7, s32[1,32]{1,0:T(1,128)} %bitcast.9, s32[2,1024]{1,0:T(2,128)} %bitcast.8), custom_call_target="tpu_custom_call" | custom-call | flops 10000000000 | bytes 10000000 | tf_op jit(solution)/shard_map/pallas_call | solution.py:527
  148.2 2.2 %copy.10 = f32[512,448]{0,1:T(8,128)} copy(f32[512,448]{0,1:T(8,128)} %bitcast.5) | data formatting | bytes 1835008
  150.3 1.5 copy.11
where the time goes:
time: 152 us
  Pallas kernels  148 us (97%)
  local copies, waits for them, and re-layouts  3.63 us (2%)
    pallas_call x1, Pallas kernels, whole_call(): pl.pallas_call(whole_kernel, out_shape=(jax.ShapeDtypeStruct((COLS, ROWS)...  148 us
    unnamed x2, local copies, waits for them, and re-layouts  3.63 us

commit v1 on v0

--- a/solution.py
+++ b/solution.py
@@ -67,9 +67,9 @@
     (1, -1), (-1, 1), (1, 1), (2, -1), (2, 1), (-1, 2), (1, 2), (2, 2),
 )
 STEPS = len(EVENTS)
-R_STEPS = (6,) + tuple(range(9, 24))
+R_STEPS = (10, 13, 14, 15, 15, 16, 16, 17, 18, 19, 19, 20, 21, 22, 22, 23)
 ORDER = 1
-ENERGY_STEP = 8
+ENERGY_STEP = 12
 SUM_LAG = 3
 RESULT_LAG = 6
 PASS_LAG = 8

time: 152 us -> 151 us (level)
  no operation moved by 1% of the time
where the time goes in v1:
time: 151 us
  Pallas kernels  147 us (97%)
  local copies, waits for them, and re-layouts  3.63 us (2%)
    pallas_call x1, Pallas kernels, whole_call(): pl.pallas_call(whole_kernel, out_shape=(jax.ShapeDtypeStruct((COLS, ROWS)...  147 us
    unnamed x2, local copies, waits for them, and re-layouts  3.63 us

profile of v1, /device:TPU:1, one launch (start us, length us, event | category | flops | bytes accessed | tf_op | source)
XLA Modules:
  0.0 150.8 jit_solution(2817843832802902549)
XLA Ops:
  0.6 146.5 %shard_map.77 = (f32[448,512]{1,0:T(8,128)}, f32[16,1024]{1,0:T(8,128)}) custom-call(bf16[128,512]{1,0:T(8,128)(2,1)} %acts_hbm.1, bf16[128,1792]{1,0:T(8,128)(2,1)} %grads_hbm.1, bf16[4096,512]{1,0:T(8,128)(2,1)} %basis_a_hbm.1, bf16[448,1792]{1,0:T(8,128)(2,1)} %bitcast.7, s32[1,32]{1,0:T(1,128)} %bitcast.9, s32[2,1024]{1,0:T(2,128)} %bitcast.8), custom_call_target="tpu_custom_call" | custom-call | flops 10000000000 | bytes 10000000 | tf_op jit(solution)/shard_map/pallas_call | solution.py:527
  147.2 2.2 %copy.10 = f32[512,448]{0,1:T(8,128)} copy(f32[512,448]{0,1:T(8,128)} %bitcast.5) | data formatting | bytes 1835008
  149.3 1.5 copy.11
